TPU v7x, 32 devices: a whole 2x2x4 slice. The times are simulated.
32 devices in a mesh: tile: 8 (over y, x, core), kern: 4 (over z).
Axes of the slice: x: 2, y: 2, z: 4, core: 2. Of those that a mesh axis runs over, the one named last changes fastest.
Arguments:
- mask_pixels: bfloat16 [1152, 9216], P(None, 'tile'), may hold values from -6 to 6
- orientation: int32 [8, 2], P('tile'), may hold values 0 or 1
- target_pattern: int32 [1152, 9216], P('kern', 'tile'), may hold values 0 or 1
- kernel_real: float32 [4, 64, 64], P('kern'), may hold values from -6 to 6
- kernel_imag: float32 [4, 64, 64], P('kern'), may hold values from -6 to 6
- eigen_weights: float32 [4], P('kern'), may hold values from 0.01 to 0.1
Outputs:
- mask_gradient: float32 [1152, 9216], P('kern', 'tile')
Inputs may be any that keep to these rules, and one draw needn't show every extreme that they name: `orientation`: 1 takes the neighbour's facing strip in order, 0 reversed; the entry for a side without neighbour is unused.
All inputs are finite; a program needn't handle non-finite values. No bound on the sum of `orientation` or of `target_pattern` on one device may be relied on, other than what follows from the above.
Results may differ from a plain program's by a relative error of at most 0.018.
Values may be sent and summed in bfloat16 or wider, within the bound.
No kernel may reach another device: no remote copies, remote signals or barrier semaphores. Data moves between devices by JAX's collectives and lax.ppermute only.
A program may use at most 64 MiB of HBM per device.

v0:
```python
import functools
import math

import jax
import jax.numpy as jnp
import ml_dtypes
import numpy as np
from jax import lax
from jax.experimental import pallas as pl
from jax.experimental.pallas import tpu as pltpu
from jax.sharding import PartitionSpec as P

N = 1152
HALO = 64
KF = 64
NE = 1280
LANES = 128
PAIR = 2 * KF
BLOCKS = N // LANES
EDGE = KF
WIDE = 3
GROUPS = BLOCKS // WIDE
MARKS = 16
BF16 = jnp.bfloat16
F32 = jnp.float32
VMEM_LIMIT = 32 * 1024 * 1024


def wave_tables():
    position = np.arange(NE)[:, None]
    frequency = np.arange(KF)[None, :] - KF // 2
    phase = np.mod(position * frequency, NE).astype(np.float64) * (2.0 * math.pi / NE)
    return np.cos(phase).astype(np.float32), np.sin(phase).astype(np.float32)


def transform_tables():
    cos, sin = wave_tables()
    full = np.concatenate([cos, sin], 1)
    mid = full[HALO : HALO + N]
    ct, st = cos[HALO : HALO + N].T, sin[HALO : HALO + N].T
    columns = np.concatenate(
        [
            np.stack([ct.reshape(KF, BLOCKS, LANES), st.reshape(KF, BLOCKS, LANES)], 2),
            np.stack([-st.reshape(KF, BLOCKS, LANES), ct.reshape(KF, BLOCKS, LANES)], 2),
        ],
        0,
    )
    to_columns = columns.transpose(1, 0, 2, 3).reshape(GROUPS, WIDE, PAIR, 2 * LANES)
    to_columns = to_columns.transpose(0, 2, 1, 3).reshape(GROUPS, PAIR, WIDE * 2 * LANES)
    from_columns = to_columns.transpose(0, 2, 1)
    low, high = full[:HALO], full[HALO + N :]
    blank = np.zeros((HALO, PAIR), np.float32)
    rims = np.stack(
        [
            np.concatenate([low[::-1], blank], 0),
            np.concatenate([low, blank], 0),
            np.concatenate([high[::-1], blank], 0),
            np.concatenate([high, blank], 0),
        ]
    )
    back = np.concatenate([cos.T, -sin.T], 0)
    back_low, back_high = back[:, :HALO], back[:, HALO + N :]
    blank = np.zeros((PAIR, HALO), np.float32)
    margins = np.stack(
        [
            np.concatenate([back_high[:, ::-1], blank], 1),
            np.concatenate([back_high, blank], 1),
            np.concatenate([blank, back_low[:, ::-1]], 1),
            np.concatenate([blank, back_low], 1),
        ]
    )
    tables = (mid, mid.T, to_columns, from_columns, rims, back[:, HALO : HALO + N], margins)
    return tuple(np.ascontiguousarray(one).astype(ml_dtypes.bfloat16) for one in tables)


def dot(a, b):
    return jnp.dot(a, b, preferred_element_type=F32)


def in_left_half(shape):
    return lax.broadcasted_iota(jnp.int32, shape, 1) < KF


def swap_halves(pair):
    return pltpu.roll(pair, KF, 1)


def destination(k, step, count):
    return k ^ step if count == 4 else (k - step) % count


def call(
    body, name, outs, args, specs, out_specs=None, scratch=(), flops=0, moved=0
):
    vmem = pl.BlockSpec(memory_space=pltpu.VMEM)
    if out_specs is None:
        out_specs = tuple(vmem for _ in outs) if isinstance(outs, tuple) else vmem
    return pl.pallas_call(
        body,
        name=name,
        out_shape=outs,
        in_specs=specs,
        out_specs=out_specs,
        scratch_shapes=list(scratch),
        compiler_params=pltpu.CompilerParams(vmem_limit_bytes=VMEM_LIMIT),
        cost_estimate=pl.CostEstimate(flops=flops, bytes_accessed=moved, transcendentals=0),
    )(*args)


def edges_body(
    mask, mid, mid_t, real, imag, weight, flags, mate, other, side, held, tall, table, pair, marks, sems
):
    odd = lax.rem(lax.axis_index("tile"), 2) == 1
    copies = [
        pltpu.make_async_copy(mid_t, table, sems.at[0]),
        pltpu.make_async_copy(mask.at[:, :LANES], held.at[:, :LANES], sems.at[1]),
        pltpu.make_async_copy(mask.at[:, N - LANES :], held.at[:, N - LANES :], sems.at[2]),
        pltpu.make_async_copy(real.at[0], pair.at[0], sems.at[3]),
        pltpu.make_async_copy(imag.at[0], pair.at[1], sems.at[4]),
        pltpu.make_async_copy(flags, marks, sems.at[5]),
    ]
    inner = pltpu.make_async_copy(
        mask.at[:, LANES : N - LANES], held.at[:, LANES : N - LANES], sems.at[6]
    )
    columns = pltpu.make_async_copy(mid, tall, sems.at[7])
    for copy in copies:
        copy.start()
    inner.start()
    columns.start()
    for copy in copies[3:]:
        copy.wait()
    scale = jnp.sqrt(jnp.full((KF, KF), 2.0 * weight[0], F32)) * (1.0 / (NE * KF))
    kernel = jnp.concatenate([pair[0] * scale, pair[1] * scale], 1).astype(BF16)
    row = lax.broadcasted_iota(jnp.int32, (16, LANES), 0)
    sides = jnp.where(row == 0, marks[0, 0].astype(F32), marks[0, 1].astype(F32)).astype(BF16)
    side[...] = kernel
    mate[EDGE : 2 * EDGE, :] = kernel
    mate[2 * EDGE :, :] = sides
    other[EDGE:, :] = sides
    for copy in copies[:3]:
        copy.wait()
    strips = jnp.concatenate([held[:, :LANES], held[:, N - LANES :]], 1)
    both = dot(table[...], strips)
    left = in_left_half((KF, LANES))
    first, last = both[:, :LANES], both[:, LANES:]
    first = jnp.where(left, first[:KF], swap_halves(first[KF:]))
    last = jnp.where(left, swap_halves(last[:KF]), last[KF:])
    mate[:EDGE, :] = jnp.where(odd, first, last).astype(BF16)
    other[:EDGE, :] = jnp.where(odd, last, first).astype(BF16)
    inner.wait()
    columns.wait()


def middle_body(mask, mid, mid_t, out):
    out[...] = dot(mid_t[...], dot(mask[...], mid[...]).astype(BF16))


def split_kernel(pair):
    left = in_left_half(pair.shape)
    other = swap_halves(pair)
    return jnp.where(left, pair, other), jnp.where(left, other, pair)


def fields_body(count, row_count, *refs):
    (flags, middle, target, mid, to_columns, from_columns, rims, own) = refs[:8]
    near_pack, *others, far_edge = refs[8 : 8 + count]
    out, a_ref, e_ref, v_ref, u_ref = refs[8 + count :]
    tile = lax.axis_index("tile")
    tiles = lax.axis_size("tile")
    left = in_left_half((KF, PAIR))
    blocks = middle[...]
    low = jnp.where(flags[0, 0] == 1, rims[1], rims[0])
    low = jnp.where(tile == 0, jnp.zeros_like(low), low)
    high = jnp.where(flags[0, 1] == 1, rims[3], rims[2])
    high = jnp.where(tile == tiles - 1, jnp.zeros_like(high), high)
    odd = lax.rem(tile, 2) == 1
    low, high = jnp.where(odd, low, high), jnp.where(odd, high, low)
    for pack, table in ((near_pack, low), (far_edge, high)):
        edge = pack[:EDGE, :].astype(F32)
        edge = jnp.concatenate([edge, swap_halves(edge)], 0).astype(BF16)
        blocks = blocks + dot(edge, table)
    top, bottom = blocks[:KF], swap_halves(blocks[KF:])
    spectrum = jnp.where(left, top - bottom, -(top + bottom))
    turned = swap_halves(spectrum)
    turned = jnp.where(left, -turned, turned)
    kernels = [own[...].astype(F32)]
    kernels.append(near_pack[EDGE : 2 * EDGE, :].astype(F32))
    kernels += [one[...].astype(F32) for one in others]
    kernels = [split_kernel(one) for one in kernels]
    begin = pl.multiple_of(lax.axis_index("kern") * row_count, row_count)
    rows = mid[pl.ds(begin, row_count), :]
    for index, (real, imag) in enumerate(kernels):
        product = real * spectrum + imag * turned
        other = swap_halves(product)
        other = jnp.where(left, -other, other)
        stacked = jnp.concatenate([product, other], 0).astype(BF16)
        a_ref[index * row_count : (index + 1) * row_count, :] = dot(rows, stacked).astype(BF16)
    step = 32 if row_count % 32 == 0 else 16
    e_ref[0] = dot(a_ref[...], to_columns[0])
    for group in range(GROUPS):
        now = group % 2
        if group + 1 < GROUPS:
            e_ref[1 - now] = dot(a_ref[...], to_columns[group + 1])
        for place in range(WIDE):
            first = (group * WIDE + place) * LANES
            halves = [slice((2 * place + half) * LANES, (2 * place + half + 1) * LANES) for half in range(2)]
            for r in range(0, row_count, step):
                total = None
                for index in range(count):
                    at = index * row_count + r
                    real, imag = (e_ref[now, at : at + step, half] for half in halves)
                    term = real * real + imag * imag
                    total = term if total is None else total + term
                wanted = target[r : r + step, first : first + LANES].astype(F32)
                decay = jnp.exp(4.0 - 2.0 * total)
                resist = pl.reciprocal(1.0 + decay, approx=True)
                slope = (resist - wanted) * (8.0 * decay) * (resist * resist)
                for index in range(count):
                    at = index * row_count + r
                    for half in halves:
                        field = e_ref[now, at : at + step, half] * slope
                        v_ref[now, at : at + step, half] = field.astype(BF16)
        part = dot(v_ref[now], from_columns[group])
        if group == 0:
            u_ref[...] = part
        else:
            u_ref[...] += part
    wide = jnp.concatenate(
        [u_ref[i * row_count : (i + 1) * row_count, :].astype(BF16) for i in range(count)], 1
    )
    waves = lax.dot_general(rows, wide, (((0,), (0,)), ((), ())), preferred_element_type=F32)
    total = None
    for index, (real, imag) in enumerate(kernels):
        wave = waves[:, index * PAIR : (index + 1) * PAIR]
        top, bottom = wave[:KF], swap_halves(wave[KF:])
        wave = jnp.where(left, top + bottom, top - bottom)
        other = swap_halves(wave)
        other = jnp.where(left, other, -other)
        term = real * wave + imag * other
        total = term if total is None else total + term
    out[...] = total.astype(BF16)


def sum_body(count, *refs):
    total = refs[0][...].astype(F32)
    for one in refs[1:count]:
        total = total + one[...].astype(F32)
    refs[count][...] = total.astype(BF16)


def row_waves(rows, pair):
    pair = pair.astype(F32)
    other = swap_halves(pair)
    other = jnp.where(in_left_half(pair.shape), -other, other)
    return dot(rows, jnp.concatenate([pair, other], 0).astype(BF16)).astype(BF16)


def own_rows(mid, row_count):
    begin = pl.multiple_of(lax.axis_index("kern") * row_count, row_count)
    return mid[pl.ds(begin, row_count), :]


def inner_body(row_count, own, mid, back, out):
    out[...] = dot(row_waves(own_rows(mid, row_count), own[...]), back[...])


def outer_body(
    row_count, near, far, near_pack, far_edge, mid, margins, begun, out, held, sems
):
    inner = pltpu.make_async_copy(
        begun.at[:, LANES : N - LANES], out.at[:, LANES : N - LANES], sems.at[2]
    )
    inner.start()
    rows = own_rows(mid, row_count)
    near_wave, far_wave = row_waves(rows, near[...]), row_waves(rows, far[...])
    odd = lax.rem(lax.axis_index("tile"), 2) == 1
    below, above = jnp.where(odd, near_wave, far_wave), jnp.where(odd, far_wave, near_wave)
    near_marks = near_pack[2 * EDGE :, :].astype(F32)
    far_marks = far_edge[EDGE:, :].astype(F32)
    low_mark = jnp.where(odd, near_marks, far_marks)[1:2]
    high_mark = jnp.where(odd, far_marks, near_marks)[0:1]
    low = jnp.where(low_mark == 1.0, margins[1].astype(F32), margins[0].astype(F32)).astype(BF16)
    high = jnp.where(high_mark == 1.0, margins[3].astype(F32), margins[2].astype(F32)).astype(BF16)
    copies = []
    for side, first, wave, table in ((0, 0, below, low), (1, N - LANES, above, high)):
        columns = slice(first, first + LANES)
        held[side] = begun[:, columns] + dot(wave, table)
        copies.append(pltpu.make_async_copy(held.at[side], out.at[:, columns], sems.at[side]))
        copies[-1].start()
    for copy in (inner, *copies):
        copy.wait()


def far_off(array):
    return pltpu.with_memory_space_constraint(array, pltpu.HBM)


def per_device(mask_pixels, orientation, target_pattern, kernel_real, kernel_imag, eigen_weights):
    tables = tuple(jnp.asarray(one) for one in transform_tables())
    mid, mid_t, to_columns, from_columns, rims, back, margins = tables
    tiles, count = lax.axis_size("tile"), lax.axis_size("kern")
    row_count = target_pattern.shape[0]
    vmem = pl.BlockSpec(memory_space=pltpu.VMEM)
    smem = pl.BlockSpec(memory_space=pltpu.SMEM)
    hbm = pl.BlockSpec(memory_space=pltpu.HBM)
    small = jax.ShapeDtypeStruct((KF, PAIR), BF16)

    mate, other, side, held, mid, mid_t = call(
        edges_body,
        "edges",
        (
            pltpu.VMEM((2 * EDGE + MARKS, LANES), BF16),
            pltpu.VMEM((EDGE + MARKS, LANES), BF16),
            pltpu.VMEM((KF, PAIR), BF16),
            pltpu.VMEM((N, N), BF16),
            pltpu.VMEM((N, PAIR), BF16),
            pltpu.VMEM((PAIR, N), BF16),
        ),
        (
            *(far_off(one) for one in (mask_pixels, mid, mid_t, kernel_real, kernel_imag)),
            eigen_weights,
            far_off(orientation),
        ),
        [hbm] * 5 + [smem, hbm],
        scratch=[
            pltpu.VMEM((2, KF, KF), F32),
            pltpu.SMEM((1, 2), jnp.int32),
            pltpu.SemaphoreType.DMA((8,)),
        ],
        flops=2 * N * LANES * PAIR * 2,
        moved=N * LANES * 4,
    )

    def swapped(move_tile, step):
        pairs = []
        for t in range(tiles):
            for k in range(count):
                pairs.append((t * count + k, move_tile(t) * count + destination(k, step, count)))
        return pairs

    def chip_mate(t):
        return t ^ 1

    def other_side(t):
        return (t + 1 if t % 2 else t - 1) % tiles

    both = ("tile", "kern")
    far_edge = lax.ppermute(other, both, swapped(other_side, 0))
    near_pack = lax.ppermute(mate, both, swapped(chip_mate, 1))
    kernels = [lax.ppermute(side, both, swapped(lambda t: t, step)) for step in range(2, count)]

    middle = call(
        middle_body,
        "middle",
        jax.ShapeDtypeStruct((PAIR, PAIR), F32),
        (held, mid, mid_t),
        [vmem] * 3,
        flops=4 * N * N * PAIR,
        moved=N * N * 2,
    )

    part = call(
        functools.partial(fields_body, count, row_count),
        "fields",
        small,
        (orientation, middle, target_pattern, mid, to_columns, from_columns, rims, side, near_pack, *kernels, far_edge),
        [smem] + [vmem] * (7 + count),
        scratch=[
            pltpu.VMEM((count * row_count, PAIR), BF16),
            pltpu.VMEM((2, count * row_count, 2 * WIDE * LANES), F32),
            pltpu.VMEM((2, count * row_count, 2 * WIDE * LANES), BF16),
            pltpu.VMEM((count * row_count, PAIR), F32),
        ],
        flops=8 * count * row_count * N * PAIR,
        moved=4 * row_count * N,
    )

    parts = [part]
    for step in range(1, count):
        pairs = [(k, destination(k, step, count)) for k in range(count)]
        parts.append(lax.ppermute(part, "kern", pairs))
    own = call(functools.partial(sum_body, count), "total", small, tuple(parts), [vmem] * count)
    near = lax.ppermute(own, "tile", [(t, chip_mate(t)) for t in range(tiles)])
    inner = [t for t in range(tiles) if 0 < t < tiles - 1]
    far = lax.ppermute(own, "tile", [(t, other_side(t)) for t in inner])
    begun = call(
        functools.partial(inner_body, row_count),
        "inner",
        pltpu.VMEM((row_count, N), F32),
        (own, mid, back),
        [vmem] * 3,
        flops=2 * row_count * PAIR * N,
        moved=4 * row_count * N,
    )
    return call(
        functools.partial(outer_body, row_count),
        "outer",
        jax.ShapeDtypeStruct((row_count, N), F32),
        (near, far, near_pack, far_edge, mid, margins, begun),
        [vmem] * 7,
        hbm,
        scratch=[
            pltpu.VMEM((2, row_count, LANES), F32),
            pltpu.SemaphoreType.DMA((3,)),
        ],
        flops=2 * row_count * PAIR * 6 * PAIR,
        moved=4 * row_count * 2 * LANES,
    )


def solution(mesh):
    in_specs = (
        P(None, "tile"),
        P("tile", None),
        P("kern", "tile"),
        P("kern", None, None),
        P("kern", None, None),
        P("kern"),
    )
    out_specs = P("kern", "tile")
    return jax.shard_map(
        per_device, mesh=mesh, in_specs=in_specs, out_specs=out_specs, check_vma=False
    )
```

profile of v0, /device:TPU:4, one launch (start us, length us, event | category | flops | bytes accessed | tf_op | source)
XLA Modules:
  0.0 30.7 jit_solution(9499986308384227071)
XLA Ops:
  0.7 2.0 %edges.1 = (bf16[144,128]{1,0:T(8,128)(2,1)S(1)}, bf16[80,128]{1,0:T(8,128)(2,1)S(1)}, bf16[64,128]{1,0:T(8,128)(2,1)S(1)}, bf16[1152,1152]{1,0:T(8,128)(2,1)S(1...) custom-call(bf16[1152,1152]{1,0:T(8,128)(2,1)} %mask.1, bf16[1152,128]{1,0:T(8,128)(2,1)} %constant.14.clone.mid, ...), custom_call_target="tpu_custom_call" | custom-call | flops 75497472 | bytes 589824 | tf_op jit(solution)/shard_map/edges/pallas_call | solution.py:98
  2.7 3.7 %collective-permute-start.2 = (bf16[64,128]{1,0:T(8,128)(2,1)S(1)}, bf16[64,128]{1,0:T(8,128)(2,1)S(1)}, u32[]{:S(2)}, u32[]{:S(2)}) collective-permute-start(bf16[64,128]{1,0:T(8,128)(2,1)S(1)} %get-tuple-element.14.refs_7_), channel_id=1, source_target_pairs={{0,3},{1,2},{2,1},{3,0},{4,7},{5,6},{6,5},{7,4},{8,11},{9,10},{10,... | collective-permute-start | bytes 49160 | tf_op jit(solution)/shard_map/ppermute | solution.py:350
  6.3 0.0 collective-permute-start.1
  6.3 0.6 %collective-permute-start.3 = (bf16[80,128]{1,0:T(8,128)(2,1)S(1)}, bf16[80,128]{1,0:T(8,128)(2,1)S(1)}, u32[]{:S(2)}, u32[]{:S(2)}) collective-permute-start(bf16[80,128]{1,0:T(8,128)(2,1)S(1)} %get-tuple-element.16), channel_id=1, source_target_pairs={{0,28},{1,29},{2,30},{3,31},{4,8},{5,9},{6,10},{7,11},{8,4},{9,5},... | collective-permute-start | bytes 61448 | tf_op jit(solution)/shard_map/ppermute | solution.py:348
  6.9 1.4 %collective-permute-start = (bf16[144,128]{1,0:T(8,128)(2,1)S(1)}, bf16[144,128]{1,0:T(8,128)(2,1)S(1)}, u32[]{:S(2)}, u32[]{:S(2)}) collective-permute-start(bf16[144,128]{1,0:T(8,128)(2,1)S(1)} %get-tuple-element.15), channel_id=1, source_target_pairs={{0,5},{1,4},{2,7},{3,6},{4,1},{5,0},{6,3},{7,2},{8,13},{9,12},{10,... | collective-permute-start | bytes 110600 | tf_op jit(solution)/shard_map/ppermute | solution.py:349
  8.3 0.0 copy-start.6
  8.3 1.1 %middle.1.refs_1_ = f32[128,128]{1,0:T(8,128)S(1)} custom-call(bf16[1152,1152]{1,0:T(8,128)(2,1)S(1)} %get-tuple-element.11.mask, bf16[1152,128]{1,0:T(8,128)(2,1)S(1)} %get-tuple-element.12.mid.refs_3_, bf16[128,1152]{1,0:T(8,128)(2,1)S(1)} %get-tuple-element.13.mid_t), custom_call_target="tpu_custom_call" | custom-call | flops 679477248 | bytes 2654208 | tf_op jit(solution)/shard_map/middle/pallas_call | solution.py:98
  9.4 0.0 copy-start
  9.4 0.0 collective-permute-done.2.refs_10_
  9.5 1.5 %collective-permute-done.1.refs_9_ = bf16[64,128]{1,0:T(8,128)(2,1)S(1)} collective-permute-done((bf16[64,128]{1,0:T(8,128)(2,1)S(1)}, bf16[64,128]{1,0:T(8,128)(2,1)S(1)}, u32[]{:S(2)}, u32[]{:S(2)}) %collective-permute-start.1) | collective-permute-done | bytes 16416 | tf_op jit(solution)/shard_map/ppermute | solution.py:350
  11.0 0.0 collective-permute-done.3.refs_11_.far_edge
  11.0 0.0 collective-permute-done.refs_8_.near_pack
  11.0 0.0 copy-done.2
  11.0 0.0 copy-done.3
  11.0 0.0 copy-done.4
  11.0 0.0 copy-done.5
  11.0 0.0 copy-done.6
  11.0 5.0 %fields.1.refs_0_ = bf16[64,128]{1,0:T(8,128)(2,1)S(1)} custom-call(s32[1,2]{1,0:T(1,128)S(1)} %copy-done.2, f32[128,128]{1,0:T(8,128)S(1)} %middle.1.refs_1_, s32[288,1152]{1,0:T(8,128)S(1)} %copy-done.3, bf16[1152,128]{1,0:T(8,128)(2,1)S(1)} %get-tuple-element.12.mid.refs_3_, bf16[3,128,768]{2,1,0:T(8,128)(2,1)S(1)} %copy-done.5, ...), custom_call_target="tpu_custom_call" | custom-call | flops 1358954496 | bytes 1327104 | tf_op jit(solution)/shard_map/fields/pallas_call | solution.py:98
  16.0 0.0 copy-start.1
  16.0 2.9 %collective-permute-start.6 = (bf16[64,128]{1,0:T(8,128)(2,1)S(1)}, bf16[64,128]{1,0:T(8,128)(2,1)S(1)}, u32[]{:S(2)}, u32[]{:S(2)}) collective-permute-start(bf16[64,128]{1,0:T(8,128)(2,1)S(1)} %fields.1.refs_0_), channel_id=1, source_target_pairs={{0,3},{1,2},{2,1},{3,0},{4,7},{5,6},{6,5},{7,4},{8,11},{9,10},{10,... | collective-permute-start | bytes 49160 | tf_op jit(solution)/shard_map/ppermute | solution.py:381
  18.9 0.0 collective-permute-start.5
  18.9 1.6 %collective-permute-start.4 = (bf16[64,128]{1,0:T(8,128)(2,1)S(1)}, bf16[64,128]{1,0:T(8,128)(2,1)S(1)}, u32[]{:S(2)}, u32[]{:S(2)}) collective-permute-start(bf16[64,128]{1,0:T(8,128)(2,1)S(1)} %fields.1.refs_0_), channel_id=1, source_target_pairs={{0,1},{1,0},{2,3},{3,2},{4,5},{5,4},{6,7},{7,6},{8,9},{9,8},{10,11... | collective-permute-start | bytes 49160 | tf_op jit(solution)/shard_map/ppermute | solution.py:381
  20.5 1.1 %collective-permute-done.6.refs_3_ = bf16[64,128]{1,0:T(8,128)(2,1)S(1)} collective-permute-done((bf16[64,128]{1,0:T(8,128)(2,1)S(1)}, bf16[64,128]{1,0:T(8,128)(2,1)S(1)}, u32[]{:S(2)}, u32[]{:S(2)}) %collective-permute-start.6) | collective-permute-done | bytes 16416 | tf_op jit(solution)/shard_map/ppermute | solution.py:381
  21.7 1.9 %collective-permute-done.5.refs_2_ = bf16[64,128]{1,0:T(8,128)(2,1)S(1)} collective-permute-done((bf16[64,128]{1,0:T(8,128)(2,1)S(1)}, bf16[64,128]{1,0:T(8,128)(2,1)S(1)}, u32[]{:S(2)}, u32[]{:S(2)}) %collective-permute-start.5) | collective-permute-done | bytes 16416 | tf_op jit(solution)/shard_map/ppermute | solution.py:381
  23.6 0.0 collective-permute-done.4.refs_1_
  23.6 1.9 %collective-permute-start.8 = (bf16[64,128]{1,0:T(8,128)(2,1)S(1)}, bf16[64,128]{1,0:T(8,128)(2,1)S(1)}, u32[]{:S(2)}, u32[]{:S(2)}) collective-permute-start(bf16[64,128]{1,0:T(8,128)(2,1)S(1)} %total.1.own), channel_id=1, source_target_pairs={{4,8},{8,4},{12,16},{16,12},{20,24},{24,20},{5,9},{9,5},{13,17},{1... | collective-permute-start | bytes 49160 | tf_op jit(solution)/shard_map/ppermute | solution.py:385
  25.5 0.7 %collective-permute-start.7 = (bf16[64,128]{1,0:T(8,128)(2,1)S(1)}, bf16[64,128]{1,0:T(8,128)(2,1)S(1)}, u32[]{:S(2)}, u32[]{:S(2)}) collective-permute-start(bf16[64,128]{1,0:T(8,128)(2,1)S(1)} %total.1.own), channel_id=1, source_target_pairs={{0,4},{4,0},{8,12},{12,8},{16,20},{20,16},{24,28},{28,24},{1,5},{5... | collective-permute-start | bytes 49160 | tf_op jit(solution)/shard_map/ppermute | solution.py:383
  26.2 0.0 copy-done
  26.2 0.5 %inner.1.begun = f32[288,1152]{1,0:T(8,128)S(1)} custom-call(bf16[64,128]{1,0:T(8,128)(2,1)S(1)} %total.1.own, bf16[1152,128]{1,0:T(8,128)(2,1)S(1)} %get-tuple-element.12.mid.refs_3_, bf16[128,1152]{1,0:T(8,128)(2,1)S(1)} %copy-done), custom_call_target="tpu_custom_call" | custom-call | flops 84934656 | bytes 1327104 | tf_op jit(solution)/shard_map/inner/pallas_call | solution.py:98
  26.7 2.8 %collective-permute-done.8.far = bf16[64,128]{1,0:T(8,128)(2,1)S(1)} collective-permute-done((bf16[64,128]{1,0:T(8,128)(2,1)S(1)}, bf16[64,128]{1,0:T(8,128)(2,1)S(1)}, u32[]{:S(2)}, u32[]{:S(2)}) %collective-permute-start.8) | collective-permute-done | bytes 16416 | tf_op jit(solution)/shard_map/ppermute | solution.py:385
  29.6 0.0 collective-permute-done.7.near
  29.6 1.1 %outer.1 = f32[288,1152]{1,0:T(8,128)} custom-call(bf16[64,128]{1,0:T(8,128)(2,1)S(1)} %collective-permute-done.7.near, bf16[64,128]{1,0:T(8,128)(2,1)S(1)} %collective-permute-done.8.far, bf16[144,128]{1,0:T(8,128)(2,1)S(1)} %collective-permute-done.refs_8_.near_pack, bf16[80,128]{1,0:T(8,128)(2,1)S(1)} %collective-permute-done.3.refs_11_.far_edge, ...), custom_call_target="tpu_custom_call" | custom-call | flops 56623104 | bytes 294912 | tf_op jit(solution)/shard_map/outer/pallas_call | solution.py:98
  (6 shorter events, 0.0 us)
Async XLA Ops:
  2.7 6.8 %collective-permute-start.2 = (bf16[64,128]{1,0:T(8,128)(2,1)S(1)}, bf16[64,128]{1,0:T(8,128)(2,1)S(1)}, u32[]{:S(2)}, u32[]{:S(2)}) collective-permute-start(bf16[64,128]{1,0:T(8,128)(2,1)S(1)} %get-tuple-element.14.refs_7_), channel_id=1, source_target_pairs={{0,3},{1,2},{2,1},{3,0},{4,7},{5,6},{6,5},{7,4},{8,11},{9,10},{10,... | collective-permute-start | bytes 49160 | tf_op jit(solution)/shard_map/ppermute | solution.py:350
  6.3 4.6 %collective-permute-start.1 = (bf16[64,128]{1,0:T(8,128)(2,1)S(1)}, bf16[64,128]{1,0:T(8,128)(2,1)S(1)}, u32[]{:S(2)}, u32[]{:S(2)}) collective-permute-start(bf16[64,128]{1,0:T(8,128)(2,1)S(1)} %get-tuple-element.14.refs_7_), channel_id=1, source_target_pairs={{0,2},{1,3},{2,0},{3,1},{4,6},{5,7},{6,4},{7,5},{8,10},{9,11},{10,... | collective-permute-start | bytes 49160 | tf_op jit(solution)/shard_map/ppermute | solution.py:350
  6.3 4.6 %collective-permute-start.3 = (bf16[80,128]{1,0:T(8,128)(2,1)S(1)}, bf16[80,128]{1,0:T(8,128)(2,1)S(1)}, u32[]{:S(2)}, u32[]{:S(2)}) collective-permute-start(bf16[80,128]{1,0:T(8,128)(2,1)S(1)} %get-tuple-element.16), channel_id=1, source_target_pairs={{0,28},{1,29},{2,30},{3,31},{4,8},{5,9},{6,10},{7,11},{8,4},{9,5},... | collective-permute-start | bytes 61448 | tf_op jit(solution)/shard_map/ppermute | solution.py:348
  6.9 4.0 %collective-permute-start = (bf16[144,128]{1,0:T(8,128)(2,1)S(1)}, bf16[144,128]{1,0:T(8,128)(2,1)S(1)}, u32[]{:S(2)}, u32[]{:S(2)}) collective-permute-start(bf16[144,128]{1,0:T(8,128)(2,1)S(1)} %get-tuple-element.15), channel_id=1, source_target_pairs={{0,5},{1,4},{2,7},{3,6},{4,1},{5,0},{6,3},{7,2},{8,13},{9,12},{10,... | collective-permute-start | bytes 110600 | tf_op jit(solution)/shard_map/ppermute | solution.py:349
  8.3 2.6 %copy-start.2 = (s32[1,2]{1,0:T(1,128)S(1)}, s32[1,2]{1,0:T(1,128)}, u32[]{:S(2)}) copy-start(s32[1,2]{1,0:T(1,128)} %refs_0_.1) | copy-start | bytes 28
  8.3 2.7 %copy-start.3 = (s32[288,1152]{1,0:T(8,128)S(1)}, s32[288,1152]{1,0:T(8,128)}, u32[]{:S(2)}) copy-start(s32[288,1152]{1,0:T(8,128)} %refs_2_.1) | copy-start | bytes 3981316
  8.3 2.7 %copy-start.4 = (bf16[3,768,128]{2,1,0:T(8,128)(2,1)S(1)}, bf16[3,768,128]{2,1,0:T(8,128)(2,1)}, u32[]{:S(2)}) copy-start(bf16[3,768,128]{2,1,0:T(8,128)(2,1)} %constant.17.clone.refs_5_) | copy-start | bytes 1769476
  8.3 2.7 %copy-start.5 = (bf16[3,128,768]{2,1,0:T(8,128)(2,1)S(1)}, bf16[3,128,768]{2,1,0:T(8,128)(2,1)}, u32[]{:S(2)}) copy-start(bf16[3,128,768]{2,1,0:T(8,128)(2,1)} %constant.16.clone.refs_4_) | copy-start | bytes 1769476
  8.3 2.7 %copy-start.6 = (bf16[4,128,128]{2,1,0:T(8,128)(2,1)S(1)}, bf16[4,128,128]{2,1,0:T(8,128)(2,1)}, u32[]{:S(2)}) copy-start(bf16[4,128,128]{2,1,0:T(8,128)(2,1)} %constant.18.clone.refs_6_) | copy-start | bytes 393220
  9.4 16.8 %copy-start = (bf16[128,1152]{1,0:T(8,128)(2,1)S(1)}, bf16[128,1152]{1,0:T(8,128)(2,1)}, u32[]{:S(2)}) copy-start(bf16[128,1152]{1,0:T(8,128)(2,1)} %constant.19.clone.back) | copy-start | bytes 884740
  16.0 13.5 %copy-start.1 = (bf16[4,128,128]{2,1,0:T(8,128)(2,1)S(1)}, bf16[4,128,128]{2,1,0:T(8,128)(2,1)}, u32[]{:S(2)}) copy-start(bf16[4,128,128]{2,1,0:T(8,128)(2,1)} %constant.20.clone.margins) | copy-start | bytes 393220
  16.0 5.6 %collective-permute-start.6 = (bf16[64,128]{1,0:T(8,128)(2,1)S(1)}, bf16[64,128]{1,0:T(8,128)(2,1)S(1)}, u32[]{:S(2)}, u32[]{:S(2)}) collective-permute-start(bf16[64,128]{1,0:T(8,128)(2,1)S(1)} %fields.1.refs_0_), channel_id=1, source_target_pairs={{0,3},{1,2},{2,1},{3,0},{4,7},{5,6},{6,5},{7,4},{8,11},{9,10},{10,... | collective-permute-start | bytes 49160 | tf_op jit(solution)/shard_map/ppermute | solution.py:381
  18.9 4.6 %collective-permute-start.5 = (bf16[64,128]{1,0:T(8,128)(2,1)S(1)}, bf16[64,128]{1,0:T(8,128)(2,1)S(1)}, u32[]{:S(2)}, u32[]{:S(2)}) collective-permute-start(bf16[64,128]{1,0:T(8,128)(2,1)S(1)} %fields.1.refs_0_), channel_id=1, source_target_pairs={{0,2},{1,3},{2,0},{3,1},{4,6},{5,7},{6,4},{7,5},{8,10},{9,11},{10,... | collective-permute-start | bytes 49160 | tf_op jit(solution)/shard_map/ppermute | solution.py:381
  18.9 4.6 %collective-permute-start.4 = (bf16[64,128]{1,0:T(8,128)(2,1)S(1)}, bf16[64,128]{1,0:T(8,128)(2,1)S(1)}, u32[]{:S(2)}, u32[]{:S(2)}) collective-permute-start(bf16[64,128]{1,0:T(8,128)(2,1)S(1)} %fields.1.refs_0_), channel_id=1, source_target_pairs={{0,1},{1,0},{2,3},{3,2},{4,5},{5,4},{6,7},{7,6},{8,9},{9,8},{10,11... | collective-permute-start | bytes 49160 | tf_op jit(solution)/shard_map/ppermute | solution.py:381
  23.6 6.0 %collective-permute-start.8 = (bf16[64,128]{1,0:T(8,128)(2,1)S(1)}, bf16[64,128]{1,0:T(8,128)(2,1)S(1)}, u32[]{:S(2)}, u32[]{:S(2)}) collective-permute-start(bf16[64,128]{1,0:T(8,128)(2,1)S(1)} %total.1.own), channel_id=1, source_target_pairs={{4,8},{8,4},{12,16},{16,12},{20,24},{24,20},{5,9},{9,5},{13,17},{1... | collective-permute-start | bytes 49160 | tf_op jit(solution)/shard_map/ppermute | solution.py:385
  25.5 4.0 %collective-permute-start.7 = (bf16[64,128]{1,0:T(8,128)(2,1)S(1)}, bf16[64,128]{1,0:T(8,128)(2,1)S(1)}, u32[]{:S(2)}, u32[]{:S(2)}) collective-permute-start(bf16[64,128]{1,0:T(8,128)(2,1)S(1)} %total.1.own), channel_id=1, source_target_pairs={{0,4},{4,0},{8,12},{12,8},{16,20},{20,16},{24,28},{28,24},{1,5},{5... | collective-permute-start | bytes 49160 | tf_op jit(solution)/shard_map/ppermute | solution.py:383
where the time goes:
time: 30.8 us; the launch traced here: 30.7 us
  starting transfers between devices  12.7 us (41%)
  Pallas kernels  9.73 us (32%)
  waiting for transfers between devices  7.4 us (24%)
  between operations  0.77 us (2%)
    pallas_call x6, Pallas kernels, call(): pl.pallas_call(body, name=name, out_shape=outs, in_specs=specs, out_specs...  9.73 us
    ppermute x3, starting transfers between devices, per_device(): parts.append(lax.ppermute(part, 'kern', pairs))  4.45 us
    ppermute x2, starting transfers between devices, per_device(): lax.ppermute(side, both, swapped(lambda t: t, step))  3.67 us
    ppermute x3, waiting for transfers between devices, per_device(): parts.append(lax.ppermute(part, 'kern', pairs))  3.07 us
    ppermute x1, waiting for transfers between devices, per_device(): far = lax.ppermute(own, 'tile', [(t, other_side(t)) for t in inner])  2.81 us
    ppermute x1, starting transfers between devices, per_device(): far = lax.ppermute(own, 'tile', [(t, other_side(t)) for t in inner])  1.92 us
    ppermute x2, waiting for transfers between devices, per_device(): lax.ppermute(side, both, swapped(lambda t: t, step))  1.51 us
    ppermute x1, starting transfers between devices, per_device(): near_pack = lax.ppermute(mate, both, swapped(chip_mate, 1))  1.4 us
  transfers between devices with their start and end apart: 9, of which 4 were waited for; matrix products, arithmetic and copies ran while one was open for 0% of the time, Pallas kernels for 5%

commit v1 on v0

--- a/solution.py
+++ b/solution.py
@@ -189,18 +189,21 @@
     kernels = [split_kernel(one) for one in kernels]
     begin = pl.multiple_of(lax.axis_index("kern") * row_count, row_count)
     rows = mid[pl.ds(begin, row_count), :]
-    for index, (real, imag) in enumerate(kernels):
+    stacks = []
+    for real, imag in kernels:
         product = real * spectrum + imag * turned
         other = swap_halves(product)
         other = jnp.where(left, -other, other)
-        stacked = jnp.concatenate([product, other], 0).astype(BF16)
-        a_ref[index * row_count : (index + 1) * row_count, :] = dot(rows, stacked).astype(BF16)
+        stacks.append(jnp.concatenate([product, other], 0).astype(BF16))
+    waves = dot(rows, jnp.concatenate(stacks, 1)).astype(BF16)
+    for index in range(count):
+        a_ref[index * row_count : (index + 1) * row_count, :] = waves[:, index * PAIR : (index + 1) * PAIR]
     step = 32 if row_count % 32 == 0 else 16
-    e_ref[0] = dot(a_ref[...], to_columns[0])
+    e_ref[0] = dot(a_ref[...], to_columns[0]).astype(BF16)
     for group in range(GROUPS):
         now = group % 2
         if group + 1 < GROUPS:
-            e_ref[1 - now] = dot(a_ref[...], to_columns[group + 1])
+            e_ref[1 - now] = dot(a_ref[...], to_columns[group + 1]).astype(BF16)
         for place in range(WIDE):
             first = (group * WIDE + place) * LANES
             halves = [slice((2 * place + half) * LANES, (2 * place + half + 1) * LANES) for half in range(2)]
@@ -209,17 +212,17 @@
                 for index in range(count):
                     at = index * row_count + r
                     real, imag = (e_ref[now, at : at + step, half] for half in halves)
-                    term = real * real + imag * imag
+                    term = (real * real + imag * imag).astype(F32)
                     total = term if total is None else total + term
                 wanted = target[r : r + step, first : first + LANES].astype(F32)
                 decay = jnp.exp(4.0 - 2.0 * total)
                 resist = pl.reciprocal(1.0 + decay, approx=True)
                 slope = (resist - wanted) * (8.0 * decay) * (resist * resist)
+                slope = slope.astype(BF16)
                 for index in range(count):
                     at = index * row_count + r
                     for half in halves:
-                        field = e_ref[now, at : at + step, half] * slope
-                        v_ref[now, at : at + step, half] = field.astype(BF16)
+                        v_ref[now, at : at + step, half] = e_ref[now, at : at + step, half] * slope
         part = dot(v_ref[now], from_columns[group])
         if group == 0:
             u_ref[...] = part
@@ -367,7 +370,7 @@
         [smem] + [vmem] * (7 + count),
         scratch=[
             pltpu.VMEM((count * row_count, PAIR), BF16),
-            pltpu.VMEM((2, count * row_count, 2 * WIDE * LANES), F32),
+            pltpu.VMEM((2, count * row_count, 2 * WIDE * LANES), BF16),
             pltpu.VMEM((2, count * row_count, 2 * WIDE * LANES), BF16),
             pltpu.VMEM((count * row_count, PAIR), F32),
         ],

time: 30.8 us -> 31.1 us (level)
  no operation moved by 1% of the time
where the time goes in v1:
time: 31.1 us; the launch traced here: 30.9 us
  starting transfers between devices  12.7 us (41%)
  Pallas kernels  10 us (32%)
  waiting for transfers between devices  7.4 us (24%)
  between operations  0.77 us (2%)
    pallas_call x6, Pallas kernels, call(): pl.pallas_call(body, name=name, out_shape=outs, in_specs=specs, out_specs...  10 us
    ppermute x3, starting transfers between devices, per_device(): parts.append(lax.ppermute(part, 'kern', pairs))  4.45 us
    ppermute x2, starting transfers between devices, per_device(): lax.ppermute(side, both, swapped(lambda t: t, step))  3.67 us
    ppermute x3, waiting for transfers between devices, per_device(): parts.append(lax.ppermute(part, 'kern', pairs))  3.07 us
    ppermute x1, waiting for transfers between devices, per_device(): far = lax.ppermute(own, 'tile', [(t, other_side(t)) for t in inner])  2.81 us
    ppermute x1, starting transfers between devices, per_device(): far = lax.ppermute(own, 'tile', [(t, other_side(t)) for t in inner])  1.92 us
    ppermute x2, waiting for transfers between devices, per_device(): lax.ppermute(side, both, swapped(lambda t: t, step))  1.51 us
    ppermute x1, starting transfers between devices, per_device(): near_pack = lax.ppermute(mate, both, swapped(chip_mate, 1))  1.4 us
  transfers between devices with their start and end apart: 9, of which 4 were waited for; matrix products, arithmetic and copies ran while one was open for 0% of the time, Pallas kernels for 5%

profile of v1, /device:TPU:4, one launch (start us, length us, event | category | flops | bytes accessed | tf_op | source)
XLA Modules:
  0.0 30.9 jit_solution(9072750988258766371)
XLA Ops:
  0.7 2.0 %edges.1 = (bf16[144,128]{1,0:T(8,128)(2,1)S(1)}, bf16[80,128]{1,0:T(8,128)(2,1)S(1)}, bf16[64,128]{1,0:T(8,128)(2,1)S(1)}, bf16[1152,1152]{1,0:T(8,128)(2,1)S(1...) custom-call(bf16[1152,1152]{1,0:T(8,128)(2,1)} %mask.1, bf16[1152,128]{1,0:T(8,128)(2,1)} %constant.14.clone.mid, ...), custom_call_target="tpu_custom_call" | custom-call | flops 75497472 | bytes 589824 | tf_op jit(solution)/shard_map/edges/pallas_call | solution.py:98
  2.7 3.7 %collective-permute-start.2 = (bf16[64,128]{1,0:T(8,128)(2,1)S(1)}, bf16[64,128]{1,0:T(8,128)(2,1)S(1)}, u32[]{:S(2)}, u32[]{:S(2)}) collective-permute-start(bf16[64,128]{1,0:T(8,128)(2,1)S(1)} %get-tuple-element.14.refs_7_), channel_id=1, source_target_pairs={{0,3},{1,2},{2,1},{3,0},{4,7},{5,6},{6,5},{7,4},{8,11},{9,10},{10,... | collective-permute-start | bytes 49160 | tf_op jit(solution)/shard_map/ppermute | solution.py:353
  6.3 0.0 collective-permute-start.1
  6.3 0.6 %collective-permute-start.3 = (bf16[80,128]{1,0:T(8,128)(2,1)S(1)}, bf16[80,128]{1,0:T(8,128)(2,1)S(1)}, u32[]{:S(2)}, u32[]{:S(2)}) collective-permute-start(bf16[80,128]{1,0:T(8,128)(2,1)S(1)} %get-tuple-element.16), channel_id=1, source_target_pairs={{0,28},{1,29},{2,30},{3,31},{4,8},{5,9},{6,10},{7,11},{8,4},{9,5},... | collective-permute-start | bytes 61448 | tf_op jit(solution)/shard_map/ppermute | solution.py:351
  6.9 1.4 %collective-permute-start = (bf16[144,128]{1,0:T(8,128)(2,1)S(1)}, bf16[144,128]{1,0:T(8,128)(2,1)S(1)}, u32[]{:S(2)}, u32[]{:S(2)}) collective-permute-start(bf16[144,128]{1,0:T(8,128)(2,1)S(1)} %get-tuple-element.15), channel_id=1, source_target_pairs={{0,5},{1,4},{2,7},{3,6},{4,1},{5,0},{6,3},{7,2},{8,13},{9,12},{10,... | collective-permute-start | bytes 110600 | tf_op jit(solution)/shard_map/ppermute | solution.py:352
  8.3 0.0 copy-start.6
  8.3 1.1 %middle.1.refs_1_ = f32[128,128]{1,0:T(8,128)S(1)} custom-call(bf16[1152,1152]{1,0:T(8,128)(2,1)S(1)} %get-tuple-element.11.mask, bf16[1152,128]{1,0:T(8,128)(2,1)S(1)} %get-tuple-element.12.mid.refs_3_, bf16[128,1152]{1,0:T(8,128)(2,1)S(1)} %get-tuple-element.13.mid_t), custom_call_target="tpu_custom_call" | custom-call | flops 679477248 | bytes 2654208 | tf_op jit(solution)/shard_map/middle/pallas_call | solution.py:98
  9.4 0.0 copy-start
  9.4 0.0 collective-permute-done.2.refs_10_
  9.5 1.5 %collective-permute-done.1.refs_9_ = bf16[64,128]{1,0:T(8,128)(2,1)S(1)} collective-permute-done((bf16[64,128]{1,0:T(8,128)(2,1)S(1)}, bf16[64,128]{1,0:T(8,128)(2,1)S(1)}, u32[]{:S(2)}, u32[]{:S(2)}) %collective-permute-start.1) | collective-permute-done | bytes 16416 | tf_op jit(solution)/shard_map/ppermute | solution.py:353
  11.0 0.0 collective-permute-done.3.refs_11_.far_edge
  11.0 0.0 collective-permute-done.refs_8_.near_pack
  11.0 0.0 copy-done.2
  11.0 0.0 copy-done.3
  11.0 0.0 copy-done.4
  11.0 0.0 copy-done.5
  11.0 0.0 copy-done.6
  11.0 5.3 %fields.1.refs_0_ = bf16[64,128]{1,0:T(8,128)(2,1)S(1)} custom-call(s32[1,2]{1,0:T(1,128)S(1)} %copy-done.2, f32[128,128]{1,0:T(8,128)S(1)} %middle.1.refs_1_, s32[288,1152]{1,0:T(8,128)S(1)} %copy-done.3, bf16[1152,128]{1,0:T(8,128)(2,1)S(1)} %get-tuple-element.12.mid.refs_3_, bf16[3,128,768]{2,1,0:T(8,128)(2,1)S(1)} %copy-done.5, ...), custom_call_target="tpu_custom_call" | custom-call | flops 1358954496 | bytes 1327104 | tf_op jit(solution)/shard_map/fields/pallas_call | solution.py:98
  16.3 0.0 copy-start.1
  16.3 2.9 %collective-permute-start.6 = (bf16[64,128]{1,0:T(8,128)(2,1)S(1)}, bf16[64,128]{1,0:T(8,128)(2,1)S(1)}, u32[]{:S(2)}, u32[]{:S(2)}) collective-permute-start(bf16[64,128]{1,0:T(8,128)(2,1)S(1)} %fields.1.refs_0_), channel_id=1, source_target_pairs={{0,3},{1,2},{2,1},{3,0},{4,7},{5,6},{6,5},{7,4},{8,11},{9,10},{10,... | collective-permute-start | bytes 49160 | tf_op jit(solution)/shard_map/ppermute | solution.py:384
  19.2 0.0 collective-permute-start.5
  19.2 1.6 %collective-permute-start.4 = (bf16[64,128]{1,0:T(8,128)(2,1)S(1)}, bf16[64,128]{1,0:T(8,128)(2,1)S(1)}, u32[]{:S(2)}, u32[]{:S(2)}) collective-permute-start(bf16[64,128]{1,0:T(8,128)(2,1)S(1)} %fields.1.refs_0_), channel_id=1, source_target_pairs={{0,1},{1,0},{2,3},{3,2},{4,5},{5,4},{6,7},{7,6},{8,9},{9,8},{10,11... | collective-permute-start | bytes 49160 | tf_op jit(solution)/shard_map/ppermute | solution.py:384
  20.8 1.1 %collective-permute-done.6.refs_3_ = bf16[64,128]{1,0:T(8,128)(2,1)S(1)} collective-permute-done((bf16[64,128]{1,0:T(8,128)(2,1)S(1)}, bf16[64,128]{1,0:T(8,128)(2,1)S(1)}, u32[]{:S(2)}, u32[]{:S(2)}) %collective-permute-start.6) | collective-permute-done | bytes 16416 | tf_op jit(solution)/shard_map/ppermute | solution.py:384
  21.9 1.9 %collective-permute-done.5.refs_2_ = bf16[64,128]{1,0:T(8,128)(2,1)S(1)} collective-permute-done((bf16[64,128]{1,0:T(8,128)(2,1)S(1)}, bf16[64,128]{1,0:T(8,128)(2,1)S(1)}, u32[]{:S(2)}, u32[]{:S(2)}) %collective-permute-start.5) | collective-permute-done | bytes 16416 | tf_op jit(solution)/shard_map/ppermute | solution.py:384
  23.8 0.0 collective-permute-done.4.refs_1_
  23.9 1.9 %collective-permute-start.8 = (bf16[64,128]{1,0:T(8,128)(2,1)S(1)}, bf16[64,128]{1,0:T(8,128)(2,1)S(1)}, u32[]{:S(2)}, u32[]{:S(2)}) collective-permute-start(bf16[64,128]{1,0:T(8,128)(2,1)S(1)} %total.1.own), channel_id=1, source_target_pairs={{4,8},{8,4},{12,16},{16,12},{20,24},{24,20},{5,9},{9,5},{13,17},{1... | collective-permute-start | bytes 49160 | tf_op jit(solution)/shard_map/ppermute | solution.py:388
  25.8 0.7 %collective-permute-start.7 = (bf16[64,128]{1,0:T(8,128)(2,1)S(1)}, bf16[64,128]{1,0:T(8,128)(2,1)S(1)}, u32[]{:S(2)}, u32[]{:S(2)}) collective-permute-start(bf16[64,128]{1,0:T(8,128)(2,1)S(1)} %total.1.own), channel_id=1, source_target_pairs={{0,4},{4,0},{8,12},{12,8},{16,20},{20,16},{24,28},{28,24},{1,5},{5... | collective-permute-start | bytes 49160 | tf_op jit(solution)/shard_map/ppermute | solution.py:386
  26.5 0.0 copy-done
  26.5 0.5 %inner.1.begun = f32[288,1152]{1,0:T(8,128)S(1)} custom-call(bf16[64,128]{1,0:T(8,128)(2,1)S(1)} %total.1.own, bf16[1152,128]{1,0:T(8,128)(2,1)S(1)} %get-tuple-element.12.mid.refs_3_, bf16[128,1152]{1,0:T(8,128)(2,1)S(1)} %copy-done), custom_call_target="tpu_custom_call" | custom-call | flops 84934656 | bytes 1327104 | tf_op jit(solution)/shard_map/inner/pallas_call | solution.py:98
  27.0 2.8 %collective-permute-done.8.far = bf16[64,128]{1,0:T(8,128)(2,1)S(1)} collective-permute-done((bf16[64,128]{1,0:T(8,128)(2,1)S(1)}, bf16[64,128]{1,0:T(8,128)(2,1)S(1)}, u32[]{:S(2)}, u32[]{:S(2)}) %collective-permute-start.8) | collective-permute-done | bytes 16416 | tf_op jit(solution)/shard_map/ppermute | solution.py:388
  29.8 0.0 collective-permute-done.7.near
  29.8 1.1 %outer.1 = f32[288,1152]{1,0:T(8,128)} custom-call(bf16[64,128]{1,0:T(8,128)(2,1)S(1)} %collective-permute-done.7.near, bf16[64,128]{1,0:T(8,128)(2,1)S(1)} %collective-permute-done.8.far, bf16[144,128]{1,0:T(8,128)(2,1)S(1)} %collective-permute-done.refs_8_.near_pack, bf16[80,128]{1,0:T(8,128)(2,1)S(1)} %collective-permute-done.3.refs_11_.far_edge, ...), custom_call_target="tpu_custom_call" | custom-call | flops 56623104 | bytes 294912 | tf_op jit(solution)/shard_map/outer/pallas_call | solution.py:98
  (6 shorter events, 0.0 us)
Async XLA Ops:
  2.7 6.8 %collective-permute-start.2 = (bf16[64,128]{1,0:T(8,128)(2,1)S(1)}, bf16[64,128]{1,0:T(8,128)(2,1)S(1)}, u32[]{:S(2)}, u32[]{:S(2)}) collective-permute-start(bf16[64,128]{1,0:T(8,128)(2,1)S(1)} %get-tuple-element.14.refs_7_), channel_id=1, source_target_pairs={{0,3},{1,2},{2,1},{3,0},{4,7},{5,6},{6,5},{7,4},{8,11},{9,10},{10,... | collective-permute-start | bytes 49160 | tf_op jit(solution)/shard_map/ppermute | solution.py:353
  6.3 4.6 %collective-permute-start.1 = (bf16[64,128]{1,0:T(8,128)(2,1)S(1)}, bf16[64,128]{1,0:T(8,128)(2,1)S(1)}, u32[]{:S(2)}, u32[]{:S(2)}) collective-permute-start(bf16[64,128]{1,0:T(8,128)(2,1)S(1)} %get-tuple-element.14.refs_7_), channel_id=1, source_target_pairs={{0,2},{1,3},{2,0},{3,1},{4,6},{5,7},{6,4},{7,5},{8,10},{9,11},{10,... | collective-permute-start | bytes 49160 | tf_op jit(solution)/shard_map/ppermute | solution.py:353
  6.3 4.6 %collective-permute-start.3 = (bf16[80,128]{1,0:T(8,128)(2,1)S(1)}, bf16[80,128]{1,0:T(8,128)(2,1)S(1)}, u32[]{:S(2)}, u32[]{:S(2)}) collective-permute-start(bf16[80,128]{1,0:T(8,128)(2,1)S(1)} %get-tuple-element.16), channel_id=1, source_target_pairs={{0,28},{1,29},{2,30},{3,31},{4,8},{5,9},{6,10},{7,11},{8,4},{9,5},... | collective-permute-start | bytes 61448 | tf_op jit(solution)/shard_map/ppermute | solution.py:351
  6.9 4.0 %collective-permute-start = (bf16[144,128]{1,0:T(8,128)(2,1)S(1)}, bf16[144,128]{1,0:T(8,128)(2,1)S(1)}, u32[]{:S(2)}, u32[]{:S(2)}) collective-permute-start(bf16[144,128]{1,0:T(8,128)(2,1)S(1)} %get-tuple-element.15), channel_id=1, source_target_pairs={{0,5},{1,4},{2,7},{3,6},{4,1},{5,0},{6,3},{7,2},{8,13},{9,12},{10,... | collective-permute-start | bytes 110600 | tf_op jit(solution)/shard_map/ppermute | solution.py:352
  8.3 2.6 %copy-start.2 = (s32[1,2]{1,0:T(1,128)S(1)}, s32[1,2]{1,0:T(1,128)}, u32[]{:S(2)}) copy-start(s32[1,2]{1,0:T(1,128)} %refs_0_.1) | copy-start | bytes 28
  8.3 2.7 %copy-start.3 = (s32[288,1152]{1,0:T(8,128)S(1)}, s32[288,1152]{1,0:T(8,128)}, u32[]{:S(2)}) copy-start(s32[288,1152]{1,0:T(8,128)} %refs_2_.1) | copy-start | bytes 3981316
  8.3 2.7 %copy-start.4 = (bf16[3,768,128]{2,1,0:T(8,128)(2,1)S(1)}, bf16[3,768,128]{2,1,0:T(8,128)(2,1)}, u32[]{:S(2)}) copy-start(bf16[3,768,128]{2,1,0:T(8,128)(2,1)} %constant.17.clone.refs_5_) | copy-start | bytes 1769476
  8.3 2.7 %copy-start.5 = (bf16[3,128,768]{2,1,0:T(8,128)(2,1)S(1)}, bf16[3,128,768]{2,1,0:T(8,128)(2,1)}, u32[]{:S(2)}) copy-start(bf16[3,128,768]{2,1,0:T(8,128)(2,1)} %constant.16.clone.refs_4_) | copy-start | bytes 1769476
  8.3 2.7 %copy-start.6 = (bf16[4,128,128]{2,1,0:T(8,128)(2,1)S(1)}, bf16[4,128,128]{2,1,0:T(8,128)(2,1)}, u32[]{:S(2)}) copy-start(bf16[4,128,128]{2,1,0:T(8,128)(2,1)} %constant.18.clone.refs_6_) | copy-start | bytes 393220
  9.4 17.1 %copy-start = (bf16[128,1152]{1,0:T(8,128)(2,1)S(1)}, bf16[128,1152]{1,0:T(8,128)(2,1)}, u32[]{:S(2)}) copy-start(bf16[128,1152]{1,0:T(8,128)(2,1)} %constant.19.clone.back) | copy-start | bytes 884740
  16.3 13.5 %copy-start.1 = (bf16[4,128,128]{2,1,0:T(8,128)(2,1)S(1)}, bf16[4,128,128]{2,1,0:T(8,128)(2,1)}, u32[]{:S(2)}) copy-start(bf16[4,128,128]{2,1,0:T(8,128)(2,1)} %constant.20.clone.margins) | copy-start | bytes 393220
  16.3 5.6 %collective-permute-start.6 = (bf16[64,128]{1,0:T(8,128)(2,1)S(1)}, bf16[64,128]{1,0:T(8,128)(2,1)S(1)}, u32[]{:S(2)}, u32[]{:S(2)}) collective-permute-start(bf16[64,128]{1,0:T(8,128)(2,1)S(1)} %fields.1.refs_0_), channel_id=1, source_target_pairs={{0,3},{1,2},{2,1},{3,0},{4,7},{5,6},{6,5},{7,4},{8,11},{9,10},{10,... | collective-permute-start | bytes 49160 | tf_op jit(solution)/shard_map/ppermute | solution.py:384
  19.2 4.6 %collective-permute-start.5 = (bf16[64,128]{1,0:T(8,128)(2,1)S(1)}, bf16[64,128]{1,0:T(8,128)(2,1)S(1)}, u32[]{:S(2)}, u32[]{:S(2)}) collective-permute-start(bf16[64,128]{1,0:T(8,128)(2,1)S(1)} %fields.1.refs_0_), channel_id=1, source_target_pairs={{0,2},{1,3},{2,0},{3,1},{4,6},{5,7},{6,4},{7,5},{8,10},{9,11},{10,... | collective-permute-start | bytes 49160 | tf_op jit(solution)/shard_map/ppermute | solution.py:384
  19.2 4.6 %collective-permute-start.4 = (bf16[64,128]{1,0:T(8,128)(2,1)S(1)}, bf16[64,128]{1,0:T(8,128)(2,1)S(1)}, u32[]{:S(2)}, u32[]{:S(2)}) collective-permute-start(bf16[64,128]{1,0:T(8,128)(2,1)S(1)} %fields.1.refs_0_), channel_id=1, source_target_pairs={{0,1},{1,0},{2,3},{3,2},{4,5},{5,4},{6,7},{7,6},{8,9},{9,8},{10,11... | collective-permute-start | bytes 49160 | tf_op jit(solution)/shard_map/ppermute | solution.py:384
  23.9 6.0 %collective-permute-start.8 = (bf16[64,128]{1,0:T(8,128)(2,1)S(1)}, bf16[64,128]{1,0:T(8,128)(2,1)S(1)}, u32[]{:S(2)}, u32[]{:S(2)}) collective-permute-start(bf16[64,128]{1,0:T(8,128)(2,1)S(1)} %total.1.own), channel_id=1, source_target_pairs={{4,8},{8,4},{12,16},{16,12},{20,24},{24,20},{5,9},{9,5},{13,17},{1... | collective-permute-start | bytes 49160 | tf_op jit(solution)/shard_map/ppermute | solution.py:388
  25.8 4.0 %collective-permute-start.7 = (bf16[64,128]{1,0:T(8,128)(2,1)S(1)}, bf16[64,128]{1,0:T(8,128)(2,1)S(1)}, u32[]{:S(2)}, u32[]{:S(2)}) collective-permute-start(bf16[64,128]{1,0:T(8,128)(2,1)S(1)} %total.1.own), channel_id=1, source_target_pairs={{0,4},{4,0},{8,12},{12,8},{16,20},{20,16},{24,28},{28,24},{1,5},{5... | collective-permute-start | bytes 49160 | tf_op jit(solution)/shard_map/ppermute | solution.py:386
